TPU v7x, 128 devices: a whole 4x4x4 slice. The times are simulated.
128 devices in a mesh: tm: 8 (over y, core), ha: 4 (over x), wa: 4 (over z).
Axes of the slice: x: 4, y: 4, z: 4, core: 2. Of those that a mesh axis runs over, the one named last changes fastest.
Arguments:
- frames: bfloat16 [32, 128, 128, 256], P('tm', 'ha', 'wa'), may hold values from -100 to 100
- history: bfloat16 [2, 128, 128, 256], P(None, 'ha', 'wa'), may hold values from -6 to 6
- cotangent: bfloat16 [32, 128, 128, 256], P('tm', 'ha', 'wa'), may hold values from -6 to 6
- space_weight: bfloat16 [3, 3, 256, 256], replicated, may hold values from -0.125 to 0.125
- time_weight: bfloat16 [3, 256, 256], replicated, may hold values from -0.21875 to 0.21875
- norm_gain: float32 [256], replicated, may hold values from 0.1 to 1.9
- norm_shift: float32 [256], replicated, may hold values from -3 to 3
Outputs:
- grad_input: bfloat16 [32, 128, 128, 256], P('tm', 'ha', 'wa')
- space_grad: float32 [3, 3, 256, 256], replicated
- time_grad: float32 [3, 256, 256], replicated
- gain_grad: float32 [256], replicated
- shift_grad: float32 [256], replicated
All inputs are finite; a program needn't handle non-finite values.
Results may differ from a plain program's by a relative error of at most 0.007.
Values may be sent and summed in bfloat16 or wider, within the bound.
A program may use at most 128 MiB of HBM per device.

v0:
```python
import functools

import jax
import jax.numpy as jnp
from jax import lax
from jax.experimental import pallas as pl
from jax.experimental.pallas import tpu as pltpu
from jax.sharding import PartitionSpec as P

MESH = pl.DeviceIdType.MESH
GROUPS = 32
EPSILON = 1e-05
DEVICES = 128
CHIPS = 64
C = 256
LOCAL = 4096
CELLS = DEVICES * LOCAL
GROUP_CELLS = CELLS * (C // GROUPS)
BF = jnp.bfloat16
F32 = jnp.float32
PIECE = 48
STEPS = ((-1, 0), (1, 0), (0, -1), (0, 1), (-1, -1), (1, -1), (-1, 1), (1, 1))


def far_first(offsets):
    def hops(offset):
        t, h, w = offset
        most = max(o[0] for o in offsets) + 1
        chips = (t + 1) // 2 if most == 8 else t
        return sum(min(n, 4 - n) for n in (chips % 4, h, w))

    return sorted(offsets[1:], key=hops, reverse=True)


def dot(a, b):
    return jnp.dot(a, b, preferred_element_type=F32)


def dot_tn(a, b):
    return lax.dot_general(a, b, (((0,), (0,)), ((), ())), preferred_element_type=F32)


def lane_group_sum(x):
    lane = lax.broadcasted_iota(jnp.int32, x.shape, 1)
    for s in (1, 2, 4):
        x = x + jnp.where((lane & s) == 0, pltpu.roll(x, 128 - s, 1), pltpu.roll(x, s, 1))
    return x


def group_sum(row):
    halves = jnp.concatenate([row[:, :128], row[:, 128:], jnp.zeros((6, 128), F32)], axis=0)
    halves = lane_group_sum(halves)
    return jnp.concatenate([halves[0:1], halves[1:2]], axis=1)


def pack_groups(a, b):
    lane = lax.broadcasted_iota(jnp.int32, (1, 128), 1) & 7
    out = jnp.where(lane == 0, a[:, :128], 0.0)
    out = jnp.where(lane == 1, a[:, 128:], out)
    out = jnp.where(lane == 2, b[:, :128], out)
    return jnp.where(lane == 3, b[:, 128:], out)


def unpack_groups(row):
    lane = lax.broadcasted_iota(jnp.int32, (1, 128), 1) & 7
    rows = [jnp.where(lane == k, row, 0.0) for k in range(4)]
    spread = lane_group_sum(jnp.concatenate(rows + [jnp.zeros((4, 128), F32)], axis=0))
    return (
        jnp.concatenate([spread[0:1], spread[1:2]], axis=1),
        jnp.concatenate([spread[2:3], spread[3:4]], axis=1),
    )


def kernel(
    frames, history, cotangent, space_weight, time_weight, gain_ref, shift_ref,
    grad_input, half_out, other_out, param_out,
    x_buf, x_past, g_buf, g_part, ext, temporal, grad_pre, grad_t, cot, result,
    w_space, w_space_t, w_time, w_time_t,
    edge, halo, halo_past, acc, sums, stat, chan_y, chan_p,
    core_out, core_in, part, scatter, plane_sum, column_part, owned, gathered, gathered_2,
    load_sem, store_sem, past_send, past_recv, halo_send, halo_recv, time_send, time_recv,
    back_send, back_recv, stat_send, stat_recv, chan_send, chan_recv,
    core_send, core_recv, big_send, big_recv, column_recv, down_recv, gather_recv, last_send, last_recv, all_here,
):
    tm, ha, wa = lax.axis_index("tm"), lax.axis_index("ha"), lax.axis_index("wa")
    core = lax.rem(tm, 2)
    height = lax.div(tm, 2)
    me = tm * 16 + ha * 4 + wa
    partner = (tm + 1 - 2 * core, ha, wa)
    spot = ha * 4 + wa
    frame_ring = [lax.rem(tm + n, 8) for n in range(8)]
    heights = [lax.rem(height + n, 4) for n in range(4)]
    rows_ring = [lax.rem(ha + n, 4) for n in range(4)]
    cols_ring = [lax.rem(wa + n, 4) for n in range(4)]
    column = [(t, ha, wa) for t in frame_ring[1:]]
    plane = [(tm, h, w) for h in rows_ring for w in cols_ring][1:]
    everyone = [
        (frame_ring[t], rows_ring[h], cols_ring[w])
        for t, h, w in far_first([(t, h, w) for t in range(8) for h in range(4) for w in range(4)])
    ]
    others = [(2 * y + core, ha, wa) for y in heights[1:]]
    around = [
        (rows_ring[h], cols_ring[w])
        for _, h, w in far_first([(0, h, w) for h in range(4) for w in range(4)])
    ]

    loads = []
    for f in (2, 3, 0, 1):
        rows = pl.ds((f % 2) * 32, 32)
        loads.append(
            pltpu.make_async_copy(
                frames.at[f], x_buf.at[1, f // 2, pl.ds(1, 32), rows], load_sem.at[f]
            )
        )
    loads.append(pltpu.make_async_copy(space_weight, w_space, load_sem.at[4]))
    loads.append(pltpu.make_async_copy(time_weight, w_time, load_sem.at[5]))
    for f in range(4):
        loads.append(
            pltpu.make_async_copy(
                cotangent.at[f], cot.at[f // 2, :, pl.ds((f % 2) * 32, 32)], load_sem.at[6 + f]
            )
        )
    past = [
        pltpu.make_async_copy(history.at[f], ext.at[0, :, pl.ds(f * 32, 32)], load_sem.at[10 + f])
        for f in range(2)
    ]
    for copy in loads:
        copy.start()

    barrier = pltpu.get_barrier_semaphore()

    for peer in column + plane:
        pl.semaphore_signal(barrier, inc=1, device_id=peer, device_id_type=MESH)

    @pl.when(tm == 0)
    def _():
        for copy in past:
            copy.start()

    def there(dh, dw):
        ok = None
        for at, by in ((ha, dh), (wa, dw)):
            if by:
                inside = (at + by >= 0) & (at + by <= 3)
                ok = inside if ok is None else ok & inside
        return ok

    def halo_places(kind, p):
        body = (x_buf, g_buf)[kind]
        edges, room = edge.at[kind], halo.at[kind]
        return (
            (body.at[1, p, 1], body.at[1, p, 33]),
            (body.at[1, p, 32], body.at[1, p, 0]),
            (edges.at[0, p], room.at[1, p, pl.ds(16, 64)]),
            (edges.at[1, p], room.at[0, p, pl.ds(16, 64)]),
            (edges.at[0, p, pl.ds(0, 16)], room.at[1, p, pl.ds(80, 16)]),
            (edges.at[0, p, pl.ds(48, 16)], room.at[1, p, pl.ds(0, 16)]),
            (edges.at[1, p, pl.ds(0, 16)], room.at[0, p, pl.ds(80, 16)]),
            (edges.at[1, p, pl.ds(48, 16)], room.at[0, p, pl.ds(0, 16)]),
        )

    def halo_copies(kind, p):
        copies = []
        for n, ((src, dst), (dh, dw)) in enumerate(zip(halo_places(kind, p), STEPS)):
            to = (tm, lax.rem(ha + dh + 4, 4), lax.rem(wa + dw + 4, 4))
            copies.append(
                pltpu.make_async_remote_copy(
                    src, dst, halo_send.at[kind, p, n], halo_recv.at[kind, p, n],
                    device_id=to, device_id_type=MESH,
                )
            )
        return copies

    def halo_zero(kind, p):
        for (_, dst), (dh, dw) in zip(halo_places(kind, p), STEPS):

            @pl.when(jnp.logical_not(there(-dh, -dw)))
            def _():
                dst[...] = jnp.zeros(dst.shape, BF)

    def halo_start(kind, p):
        for copy, (dh, dw) in zip(halo_copies(kind, p), STEPS):
            pl.when(there(dh, dw))(copy.start)

    def halo_wait(kind, p):
        for copy, (dh, dw) in zip(halo_copies(kind, p), STEPS):
            pl.when(there(-dh, -dw))(copy.wait_recv)

    def halo_sent(kind, p):
        for copy, (dh, dw) in zip(halo_copies(kind, p), STEPS):
            pl.when(there(dh, dw))(copy.wait_send)

    row = lax.broadcasted_iota(jnp.int32, (32, 512), 0)
    col = lax.broadcasted_iota(jnp.int32, (32, 512), 1)
    pick = ((row & 15) * 32 + jnp.where(row < 16, 0, 31) == col).astype(F32).astype(BF)

    def take_edges(kind, p):
        body = (x_buf, g_buf)[kind]
        for g in range(4):
            both = dot(pick, body[1, p, 1 + 8 * g : 9 + 8 * g].reshape(512, C)).astype(BF)
            edge[kind, 0, p, 16 * g : 16 * g + 16] = both[:16]
            edge[kind, 1, p, 16 * g : 16 * g + 16] = both[16:]

    place = lax.broadcasted_iota(jnp.int32, (64, C), 0)

    def shift_row(body, h, low, high, v):
        x = body[1, h].astype(F32)
        a = pltpu.roll(x, 1, 0)
        a = jnp.where(place == 0, low[2 * v : 2 * v + 1], a)
        a = jnp.where(place == 32, low[2 * v + 1 : 2 * v + 2], a)
        body[0, h] = a.astype(BF)
        b = pltpu.roll(x, 63, 0)
        b = jnp.where(place == 31, high[2 * v : 2 * v + 1], b)
        b = jnp.where(place == 63, high[2 * v + 1 : 2 * v + 2], b)
        body[2, h] = b.astype(BF)

    def shift_all(body, room):
        for h, at, v in ((0, 0, 7), (33, 80, 0)):
            low = room[0, at : at + 16].astype(F32)
            high = room[1, at : at + 16].astype(F32)
            shift_row(body, h, low, high, v)

        @pl.loop(0, 4)
        def _(g):
            at = pl.ds(pl.multiple_of(16 * g + 16, 16), 16)
            low = room[0, at].astype(F32)
            high = room[1, at].astype(F32)
            for v in range(8):
                shift_row(body, 8 * g + 1 + v, low, high, v)

    def conv(kind, p, h, count, weights):
        body = (x_buf, g_buf)[kind]
        lhs = jnp.concatenate(
            [
                body[j, p, pl.ds(h + i, count)].reshape(count * 64, C)
                for i in range(3)
                for j in range(3)
            ],
            axis=1,
        )
        return dot(lhs, weights[...]).astype(BF).reshape(count, 64, C)

    for kind in range(2):
        for p in range(2):
            halo_zero(kind, p)

    @pl.when(tm == 7)
    def _():
        grad_t[2] = jnp.zeros((32, 64, C), BF)

    @pl.when(tm == 0)
    def _():
        x_past[...] = jnp.zeros(x_past.shape, BF)

    loads[0].wait()
    loads[1].wait()
    take_edges(0, 1)
    loads[2].wait()
    loads[3].wait()
    take_edges(0, 0)
    pl.semaphore_wait(barrier, len(column + plane))
    for peer in column:
        pl.semaphore_signal(all_here, inc=1, device_id=peer, device_id_type=MESH)
    halo_start(0, 1)
    halo_start(0, 0)
    loads[4].wait()
    loads[5].wait()
    for t in range(9):
        w_space_t[t * C : (t + 1) * C] = w_space[(8 - t) * C : (9 - t) * C].T
    for k in range(3):
        w_time_t[k * C : (k + 1) * C] = w_time[k * C : (k + 1) * C].T

    def to_next(n):
        part_rows = pl.ds(n * 8, 8)
        return pltpu.make_async_remote_copy(
            ext.at[2, part_rows], ext.at[0, part_rows], time_send.at[n], time_recv.at[n],
            device_id=(lax.rem(tm + 1, 8), ha, wa), device_id_type=MESH,
        )

    halo_wait(0, 1)
    shift_all(x_buf.at[:, 1], halo.at[0, :, 1])
    for n in range(4):
        ext[2, 8 * n : 8 * n + 8] = conv(0, 1, 8 * n, 8, w_space)
        pl.when(tm < 7)(to_next(n).start)
    halo_wait(0, 0)
    shift_all(x_buf.at[:, 0], halo.at[0, :, 0])
    for n in range(2):
        ext[1, 16 * n : 16 * n + 16] = conv(0, 0, 16 * n, 16, w_space)

    def between(a, b):
        return jnp.concatenate([a[:, 32:], b[:, :32]], axis=1)

    def temporal_pair(q):
        sums[0:1] = jnp.zeros((1, C), F32)

        @pl.loop(0, 2)
        def _(n):
            s = pl.ds(n * 16, 16)
            a, b = ext[q, s], ext[q + 1, s]
            lhs = jnp.concatenate(
                [v.reshape(1024, C) for v in (b, between(a, b), a)], axis=1
            )
            t = dot(lhs, w_time[...])
            temporal[q, s] = t.reshape(16, 64, C)
            sums[0:1] += jnp.sum(t, axis=0, keepdims=True)

        mean = group_sum(sums[0:1]) * (1.0 / (2048 * 8))
        sums[1:2] = jnp.zeros((1, C), F32)

        @pl.loop(0, 8)
        def _(n):
            apart = temporal[q, pl.ds(n * 4, 4)].reshape(256, C) - mean
            sums[1:2] += jnp.sum(apart * apart, axis=0, keepdims=True)

        return mean, group_sum(sums[1:2])

    mean_1, square_1 = temporal_pair(1)
    pl.when(tm == 0)(past[0].wait)
    pl.when(tm == 0)(past[1].wait)
    for n in range(4):
        pl.when(tm > 0)(to_next(n).wait_recv)
    mean_0, square_0 = temporal_pair(0)
    mean_here = 0.5 * (mean_0 + mean_1)
    square_here = square_0 + square_1 + (0.5 * 2048 * 8) * jnp.square(mean_0 - mean_1)

    def share_start(n, packed):
        stat[n, me] = packed

        for peer in everyone:
            pltpu.make_async_remote_copy(
                stat.at[n, me], stat.at[n, me], stat_send.at[n], stat_recv.at[n],
                device_id=peer, device_id_type=MESH,
            ).start()

    def share_wait(n, sem):
        most = stat.at[n, pl.ds(0, DEVICES - 1)]
        pltpu.make_async_copy(most, most, sem.at[n]).wait()

    ahead = (lax.rem(tm + 1, 8), ha, wa)
    frames_on = [
        pltpu.make_async_remote_copy(
            src, dst, past_send.at[n], past_recv.at[n], device_id=ahead, device_id_type=MESH
        )
        for n, (src, dst) in enumerate(
            ((x_buf.at[1, 1], x_past.at[1]), (halo.at[0, :, 1], halo_past))
        )
    ]
    pl.semaphore_wait(all_here, len(column))
    share_start(0, pack_groups(mean_here, square_here))
    for copy in frames_on:
        pl.when(tm < 7)(copy.start)
    share_wait(0, stat_recv)
    all_stat = stat[0]
    average = jnp.sum(all_stat, axis=0) * (1.0 / DEVICES)
    total = jnp.sum(all_stat, axis=0)
    spread = jnp.sum(jnp.square(all_stat - average), axis=0) * (LOCAL * 8.0)
    mean, spread = unpack_groups(average)[0], unpack_groups(spread)[0]
    variance = (unpack_groups(total)[1] + spread) * (1.0 / GROUP_CELLS)
    inv_std = lax.rsqrt(variance + EPSILON)
    gain, norm_shift = gain_ref[...], shift_ref[...]

    for copy in loads[6:]:
        copy.wait()
    sums[2:4] = jnp.zeros((2, C), F32)
    for q in range(2):

        @pl.loop(0, 16)
        def _(n):
            s = pl.ds(n * 2, 2)
            normal = (temporal[q, s].reshape(128, C) - mean) * inv_std
            value = normal * gain + norm_shift
            logistic = 0.5 + 0.5 * jnp.tanh(0.5 * value)
            slope = logistic * (1.0 + value * (1.0 - logistic))
            g = cot[q, s].reshape(128, C).astype(F32) * slope
            temporal[q, s] = normal.reshape(2, 64, C)
            grad_pre[q, s] = g.reshape(2, 64, C)
            sums[2:3] += jnp.sum(g, axis=0, keepdims=True)
            sums[3:4] += jnp.sum(g * normal, axis=0, keepdims=True)

    shift_here, gain_here = sums[2:3], sums[3:4]
    share_start(1, pack_groups(group_sum(gain * shift_here), group_sum(gain * gain_here)))

    chan_here = jnp.concatenate(
        [shift_here[:, :128], shift_here[:, 128:], gain_here[:, :128], gain_here[:, 128:]], axis=0
    )

    def chan_copy(step, i):
        if step == 0:
            return pltpu.make_async_remote_copy(
                chan_y.at[tm], chan_y.at[tm], chan_send.at[0], chan_recv.at[0],
                device_id=column[i - 1], device_id_type=MESH,
            )
        at = ha * 4 + wa
        return pltpu.make_async_remote_copy(
            chan_p.at[at], chan_p.at[at], chan_send.at[1], chan_recv.at[1],
            device_id=plane[i - 1], device_id_type=MESH,
        )

    def chan_start(step, value):
        if step == 0:
            chan_y[tm] = value
        else:
            chan_p[ha * 4 + wa] = value
        for i in range(1, (8, 16)[step]):
            chan_copy(step, i).start()

    def chan_wait(step, sem):
        most = (chan_y, chan_p)[step].at[pl.ds(0, (7, 15)[step])]
        pltpu.make_async_copy(most, most, sem.at[step]).wait()

    chan_start(0, chan_here)

    @pl.when(tm > 0)
    def _():
        for copy in frames_on:
            copy.wait_recv()
        shift_all(x_past, halo_past)

    share_wait(1, stat_recv)
    first, second = unpack_groups(jnp.sum(stat[1], axis=0))
    scale_g = inv_std * gain
    offset = inv_std * first * (1.0 / GROUP_CELLS)
    scale_n = inv_std * second * (1.0 / GROUP_CELLS)

    def to_previous(n):
        part_rows = pl.ds(n * 8, 8)
        return pltpu.make_async_remote_copy(
            grad_t.at[0, part_rows], grad_t.at[2, part_rows], back_send.at[n], back_recv.at[n],
            device_id=(lax.rem(tm + 7, 8), ha, wa), device_id_type=MESH,
        )

    for q in range(2):
        for n in range(4):
            for half in range(2):
                s = pl.ds(n * 8 + half * 4, 4)
                g = grad_pre[q, s].reshape(256, C) * scale_g - offset
                g = g - temporal[q, s].reshape(256, C) * scale_n
                grad_t[q, s] = g.astype(BF).reshape(4, 64, C)
            if q == 0:
                pl.when(tm > 0)(to_previous(n).start)

    for k in range(3):
        total_k = None
        for q in range(2):
            for n in range(2):
                s = slice(n * 16, n * 16 + 16)
                if k == 0:
                    e = ext[q + 1, s]
                elif k == 1:
                    e = between(ext[q, s], ext[q + 1, s])
                else:
                    e = ext[q, s]
                d = dot_tn(e.reshape(1024, C), grad_t[q, s].reshape(1024, C))
                total_k = d if total_k is None else total_k + d
        acc[0, 9 + k] = total_k[:, :128]
        acc[1, 9 + k] = total_k[:, 128:]

    chan_wait(0, chan_recv)
    chan_start(1, jnp.sum(chan_y[...], axis=0))

    def features_back(p):
        @pl.loop(0, 2)
        def _(n):
            s = pl.ds(n * 16, 16)
            a, b = grad_t[p, s], grad_t[p + 1, s]
            lhs = jnp.concatenate(
                [v.reshape(1024, C) for v in (a, between(a, b), b)], axis=1
            )
            g_buf[1, p, pl.ds(n * 16 + 1, 16)] = (
                dot(lhs, w_time_t[...]).astype(BF).reshape(16, 64, C)
            )

        take_edges(1, p)
        halo_start(1, p)

    def features_parts():
        @pl.loop(0, 2)
        def _(n):
            s = pl.ds(n * 16, 16)
            a, b = grad_t[1, s], grad_t[0, s]
            none = jnp.zeros((16, 32, C), BF)
            for m, (lhs, rhs) in enumerate(
                (
                    ((a, jnp.concatenate([a[:, 32:], none], axis=1)), w_time_t[: 2 * C]),
                    ((jnp.concatenate([none, b[:, :32]], axis=1), b), w_time_t[C:]),
                )
            ):
                lhs = jnp.concatenate([v.reshape(1024, C) for v in lhs], axis=1)
                g_part[m, s] = dot(lhs, rhs).astype(BF).reshape(16, 64, C)

    def space_tap(t):
        i, j = t // 3, lax.rem(t, 3)
        rows = pl.ds(i, 32)
        pairs = (
            (x_buf[j, 0, rows], g_buf[1, 0, 1:33]),
            (x_buf[j, 1, rows], g_part[0]),
            (x_past[j, rows], g_part[1]),
        )
        return sum(dot_tn(x.reshape(2048, C), g.reshape(2048, C)) for x, g in pairs)

    stores = [
        pltpu.make_async_copy(
            result.at[f // 2, :, pl.ds((f % 2) * 32, 32)], grad_input.at[f], store_sem.at[f]
        )
        for f in range(4)
    ]

    def input_back(p):
        halo_wait(1, p)
        shift_all(g_buf.at[:, p], halo.at[1, :, p])
        for n in range(2):
            result[p, 16 * n : 16 * n + 16] = conv(1, p, 16 * n, 16, w_space_t)
        stores[2 * p].start()
        stores[2 * p + 1].start()

    def core_copy(t):
        return pltpu.make_async_remote_copy(
            core_out.at[t], core_in.at[t], core_send.at[t], core_recv.at[t],
            device_id=partner, device_id_type=MESH,
        )

    def core_start(t):
        core_out[t] = acc[1 - core, t].astype(BF)
        core_copy(t).start()

    def rows_of(index):
        return pl.ds(pl.multiple_of(index * PIECE, PIECE), PIECE)

    def core_sum(group):
        for t in range(3 * group, 3 * group + 3):
            core_copy(t).wait_recv()
            part[t * 256 : t * 256 + 256] = (acc[core, t] + core_in[t].astype(F32)).astype(BF)

    def scatter_start(group):
        core_sum(group)
        for h, w in around:
            pltpu.make_async_remote_copy(
                part.at[rows_of(group * 16 + h * 4 + w)], scatter.at[group * 16 + spot],
                big_send.at[0], big_recv.at[group],
                device_id=(tm, h, w), device_id_type=MESH,
            ).start()
        scatter[group * 16 + spot] = part[rows_of(group * 16 + spot)]

    def big_wait(buf, sem, count):
        most = buf.at[pl.ds(0, count)]
        pltpu.make_async_copy(most, most, sem).wait()

    def up_copy(group):
        return pltpu.make_async_remote_copy(
            plane_sum.at[group], column_part.at[height], big_send.at[1], column_recv.at[0],
            device_id=(2 * group + core, ha, wa), device_id_type=MESH,
        )

    def add_plane(group):
        big_wait(scatter, big_recv.at[group], 15)
        rows = scatter[16 * group : 16 * group + 16].astype(F32)
        plane_sum[group] = jnp.sum(rows, axis=0).astype(BF)

        @pl.when(height == group)
        def _():
            column_part[group] = plane_sum[group]

        pl.when(height != group)(up_copy(group).start)

    def down_copy(to):
        return pltpu.make_async_remote_copy(
            owned, gathered.at[height * 16 + spot], big_send.at[2], down_recv.at[height],
            device_id=to, device_id_type=MESH,
        )

    def add_column():
        big_wait(column_part, column_recv.at[0], 3)
        owned[...] = jnp.sum(column_part[...].astype(F32), axis=0).astype(BF)
        for to in others:
            down_copy(to).start()
        gathered[height * 16 + spot] = owned[...]

    def spread(group):
        place_here = gathered.at[group * 16 + spot]

        @pl.when(height != group)
        def _():
            pltpu.make_async_copy(place_here, place_here, down_recv.at[group]).wait()

        for h, w in around:
            pltpu.make_async_remote_copy(
                place_here, place_here, big_send.at[3], gather_recv.at[group],
                device_id=(tm, h, w), device_id_type=MESH,
            ).start()

    def swap_copy(group):
        span = pl.ds(group * 16, 16)
        return pltpu.make_async_remote_copy(
            gathered.at[span], gathered_2.at[span], last_send.at[group], last_recv.at[group],
            device_id=partner, device_id_type=MESH,
        )

    def keep_copies(group):
        span = pl.ds(group * 16, 16)
        return (
            pltpu.make_async_copy(gathered.at[span], half_out.at[span], store_sem.at[4 + group]),
            pltpu.make_async_copy(gathered_2.at[span], other_out.at[span], store_sem.at[8 + group]),
        )

    def taps(low, high):
        @pl.loop(low, high)
        def _(t):
            d = space_tap(t)
            acc[0, t] = d[:, :128]
            acc[1, t] = d[:, 128:]
            core_start(t)

    for t in range(9, 12):
        core_start(t)
    features_back(0)
    features_parts()

    scatter_start(3)
    taps(0, 4)
    scatter_start(0)
    add_plane(3)
    taps(4, 7)
    scatter_start(1)
    add_plane(0)
    taps(7, 9)
    for n in range(4):
        pl.when(tm < 7)(to_previous(n).wait_recv)
    features_back(1)
    scatter_start(2)
    pl.when((height == 3) | (height == 0))(add_column)
    add_plane(1)
    input_back(0)
    add_plane(2)
    pl.when(height == 1)(add_column)
    spread(3)
    spread(0)
    input_back(1)
    pl.when(height == 2)(add_column)
    spread(1)
    spread(2)

    grad_scale = float(CELLS) ** -0.5
    chan_wait(1, chan_recv)
    param_out[...] = jnp.sum(chan_p[...], axis=0) * grad_scale

    for group in (3, 0, 1, 2):
        big_wait(gathered, gather_recv.at[group], 15)
        swap_copy(group).start()
        keep_copies(group)[0].start()
    for group in (3, 0, 1, 2):
        swap_copy(group).wait_recv()
        keep_copies(group)[1].start()

    for kind in range(2):
        for p in range(2):
            halo_sent(kind, p)
    for n in range(4):
        pl.when(tm < 7)(to_next(n).wait_send)
        pl.when(tm > 0)(to_previous(n).wait_send)
    for copy in frames_on:
        pl.when(tm < 7)(copy.wait_send)
    share_wait(0, stat_send)
    share_wait(1, stat_send)
    chan_wait(0, chan_send)
    chan_wait(1, chan_send)

    @pl.loop(0, 12)
    def _(t):
        core_copy(t).wait_send()

    big_wait(scatter, big_send.at[0], 60)
    big_wait(plane_sum, big_send.at[1], 3)
    big_wait(plane_sum, big_send.at[2], 3)
    big_wait(gathered, big_send.at[3], 60)
    for group in range(4):
        swap_copy(group).wait_send()
        for copy in keep_copies(group):
            copy.wait()
    for copy in stores:
        copy.wait()


def finish(
    grad_in, half, other, params, grad_input, space_out, time_out, gain_out, shift_out
):
    core = lax.rem(lax.axis_index("tm"), 2)
    step = pl.program_id(0)
    grad_scale = float(CELLS) ** -0.5
    grad_input[...] = grad_in[...]
    shift_out[...] = jnp.concatenate([params[0:1], params[1:2]], axis=1)
    gain_out[...] = jnp.concatenate([params[2:3], params[3:4]], axis=1)

    def put(out):
        a = half[...].reshape(3, C, 128).astype(F32) * grad_scale
        b = other[...].reshape(3, C, 128).astype(F32) * grad_scale
        out[:, :, :128] = jnp.where(core == 0, a, b)
        out[:, :, 128:] = jnp.where(core == 0, b, a)

    pl.when(step < 3)(functools.partial(put, space_out))
    pl.when(step == 3)(functools.partial(put, time_out))


def body(frames, history, cotangent, space_weight, time_weight, norm_gain, norm_shift):
    hbm = pl.BlockSpec(memory_space=pl.ANY)
    vmem = pl.BlockSpec(memory_space=pltpu.VMEM)
    dma = pltpu.SemaphoreType.DMA
    chunks = jax.ShapeDtypeStruct((CHIPS, PIECE, 128), BF)
    grad_input, half, other, params = pl.pallas_call(
        kernel,
        out_shape=(
            jax.ShapeDtypeStruct((4, 32, 32, C), BF),
            chunks,
            chunks,
            jax.ShapeDtypeStruct((4, 128), F32),
        ),
        in_specs=[hbm] * 5 + [vmem] * 2,
        out_specs=(hbm, hbm, hbm, vmem),
        scratch_shapes=[
            pltpu.VMEM((3, 2, 34, 64, C), BF),
            pltpu.VMEM((3, 34, 64, C), BF),
            pltpu.VMEM((3, 2, 34, 64, C), BF),
            pltpu.VMEM((2, 32, 64, C), BF),
            pltpu.VMEM((3, 32, 64, C), BF),
            pltpu.VMEM((2, 32, 64, C), F32),
            pltpu.VMEM((2, 32, 64, C), F32),
            pltpu.VMEM((3, 32, 64, C), BF),
            pltpu.VMEM((2, 32, 64, C), BF),
            pltpu.VMEM((2, 32, 64, C), BF),
            pltpu.VMEM((9 * C, C), BF),
            pltpu.VMEM((9 * C, C), BF),
            pltpu.VMEM((3 * C, C), BF),
            pltpu.VMEM((3 * C, C), BF),
            pltpu.VMEM((2, 2, 2, 64, C), BF),
            pltpu.VMEM((2, 2, 2, 96, C), BF),
            pltpu.VMEM((2, 96, C), BF),
            pltpu.VMEM((2, 12, C, 128), F32),
            pltpu.VMEM((8, C), F32),
            pltpu.VMEM((2, DEVICES, 1, 128), F32),
            pltpu.VMEM((8, 4, 128), F32),
            pltpu.VMEM((16, 4, 128), F32),
            pltpu.VMEM((12, C, 128), BF),
            pltpu.VMEM((12, C, 128), BF),
            pltpu.VMEM((12 * C, 128), BF),
            pltpu.VMEM((CHIPS, PIECE, 128), BF),
            pltpu.VMEM((4, PIECE, 128), BF),
            pltpu.VMEM((4, PIECE, 128), BF),
            pltpu.VMEM((PIECE, 128), BF),
            pltpu.VMEM((CHIPS, PIECE, 128), BF),
            pltpu.VMEM((CHIPS, PIECE, 128), BF),
            dma((12,)),
            dma((12,)),
            dma((2,)),
            dma((2,)),
            dma((2, 2, 8)),
            dma((2, 2, 8)),
            dma((4,)),
            dma((4,)),
            dma((4,)),
            dma((4,)),
            dma((2,)),
            dma((2,)),
            dma((2,)),
            dma((2,)),
            dma((12,)),
            dma((12,)),
            dma((4,)),
            dma((4,)),
            dma((1,)),
            dma((4,)),
            dma((4,)),
            dma((4,)),
            dma((4,)),
            pltpu.SemaphoreType.REGULAR,
        ],
        compiler_params=pltpu.CompilerParams(
            collective_id=0, has_side_effects=True, vmem_limit_bytes=58 << 20
        ),
        name="decoder_block_backward",
    )(
        frames,
        history,
        cotangent,
        space_weight.reshape(9 * C, C),
        time_weight.reshape(3 * C, C),
        norm_gain.reshape(1, C),
        norm_shift.reshape(1, C),
    )
    grad_input, space_grad, time_grad, gain_grad, shift_grad = pl.pallas_call(
        finish,
        out_shape=(
            jax.ShapeDtypeStruct((4, 32, 32, C), BF),
            jax.ShapeDtypeStruct((9, C, C), F32),
            jax.ShapeDtypeStruct((3, C, C), F32),
            jax.ShapeDtypeStruct((1, C), F32),
            jax.ShapeDtypeStruct((1, C), F32),
        ),
        grid=(4,),
        in_specs=[
            pl.BlockSpec((1, 32, 32, C), lambda n: (n, 0, 0, 0)),
            pl.BlockSpec((16, PIECE, 128), lambda n: (n, 0, 0)),
            pl.BlockSpec((16, PIECE, 128), lambda n: (n, 0, 0)),
            pl.BlockSpec((4, 128), lambda n: (0, 0)),
        ],
        out_specs=(
            pl.BlockSpec((1, 32, 32, C), lambda n: (n, 0, 0, 0)),
            pl.BlockSpec((3, C, C), lambda n: (jnp.minimum(n, 2), 0, 0)),
            pl.BlockSpec((3, C, C), lambda n: (0, 0, 0)),
            pl.BlockSpec((1, C), lambda n: (0, 0)),
            pl.BlockSpec((1, C), lambda n: (0, 0)),
        ),
        compiler_params=pltpu.CompilerParams(vmem_limit_bytes=58 << 20),
        name="scale_and_store",
    )(grad_input, half, other, params)
    return (
        grad_input,
        space_grad.reshape(3, 3, C, C),
        time_grad,
        gain_grad.reshape(C),
        shift_grad.reshape(C),
    )


def solution(mesh):
    split = P("tm", "ha", "wa", None)
    in_specs = (split, P(None, "ha", "wa", None), split, P(), P(), P(), P())
    out_specs = (split, P(), P(), P(), P())
    return jax.shard_map(body, mesh=mesh, in_specs=in_specs, out_specs=out_specs, check_vma=False)
```

profile of v0, /device:TPU:1, one launch (start us, length us, event | category | flops | bytes accessed | tf_op | source)
XLA Modules:
  0.0 91.0 jit_solution(10912267111159907959)
XLA Ops:
  0.6 84.9 %decoder_block_backward.1 = (bf16[4,32,32,256]{3,2,1,0:T(8,128)(2,1)}, bf16[64,48,128]{2,1,0:T(8,128)(2,1)}, bf16[64,48,128]{2,1,0:T(8,128)(2,1)}, f32[4,128]{1,0:T(4,128)}) custom-call(bf16[4,32,32,256]{3,2,1,0:T(8,128)(2,1)} %frames.1, bf16[2,32,32,256]{3,2,1,0:T(8,128)(2,1)} %history.1, bf16[4,32,32,256]{3,2,1,0:T(8,128)(2,1)} %cotangent.1, ...), custom_call_target="tpu_custom_call" | custom-call | tf_op jit(solution)/shard_map/decoder_block_backward/pallas_call | solution.py:708
  85.5 5.3 %scale_and_store.1 = (bf16[4,32,32,256]{3,2,1,0:T(8,128)(2,1)}, f32[9,256,256]{2,1,0:T(8,128)}, f32[3,256,256]{2,1,0:T(8,128)}, f32[1,256]{1,0:T(1,128)}, f32[1,256]{1,0:T(1,128)}) custom-call(bf16[4,32,32,256]{3,2,1,0:T(8,128)(2,1)} %get-tuple-element.14.grad_in, bf16[64,48,128]{2,1,0:T(8,128)(2,1)} %get-tuple-element.15.half, ...), custom_call_target="tpu_custom_call" | custom-call | tf_op jit(solution)/shard_map/scale_and_store/pallas_call | solution.py:788
where the time goes:
time: 91.2 us; the launch traced here: 91 us
  Pallas kernels  90.2 us (99%)
    pallas_call x1, Pallas kernels, body(): pl.pallas_call(kernel, out_shape=(jax.ShapeDtypeStruct((4, 32, 32, C), BF...  84.9 us
    pallas_call x1, Pallas kernels, body(): pl.pallas_call(finish, out_shape=(jax.ShapeDtypeStruct((4, 32, 32, C), BF...  5.28 us

commit v1 on v0

--- a/solution.py
+++ b/solution.py
@@ -77,10 +77,10 @@
     x_buf, x_past, g_buf, g_part, ext, temporal, grad_pre, grad_t, cot, result,
     w_space, w_space_t, w_time, w_time_t,
     edge, halo, halo_past, acc, sums, stat, chan_y, chan_p,
-    core_out, core_in, part, scatter, plane_sum, column_part, owned, gathered, gathered_2,
+    core_out, core_in, part, scatter, plane_sum, column_part, gathered, gathered_2,
     load_sem, store_sem, past_send, past_recv, halo_send, halo_recv, time_send, time_recv,
     back_send, back_recv, stat_send, stat_recv, chan_send, chan_recv,
-    core_send, core_recv, big_send, big_recv, column_recv, down_recv, gather_recv, last_send, last_recv, all_here,
+    core_send, core_recv, big_send, big_recv, column_recv, gather_recv, last_send, last_recv, all_here,
 ):
     tm, ha, wa = lax.axis_index("tm"), lax.axis_index("ha"), lax.axis_index("wa")
     core = lax.rem(tm, 2)
@@ -505,11 +505,13 @@
         for f in range(4)
     ]
 
-    def input_back(p):
+    def input_back(p, halfway=None):
         halo_wait(1, p)
         shift_all(g_buf.at[:, p], halo.at[1, :, p])
         for n in range(2):
             result[p, 16 * n : 16 * n + 16] = conv(1, p, 16 * n, 16, w_space_t)
+            if n == 0 and halfway is not None:
+                halfway()
         stores[2 * p].start()
         stores[2 * p + 1].start()
 
@@ -545,46 +547,24 @@
         most = buf.at[pl.ds(0, count)]
         pltpu.make_async_copy(most, most, sem).wait()
 
-    def up_copy(group):
-        return pltpu.make_async_remote_copy(
-            plane_sum.at[group], column_part.at[height], big_send.at[1], column_recv.at[0],
-            device_id=(2 * group + core, ha, wa), device_id_type=MESH,
-        )
-
     def add_plane(group):
         big_wait(scatter, big_recv.at[group], 15)
         rows = scatter[16 * group : 16 * group + 16].astype(F32)
         plane_sum[group] = jnp.sum(rows, axis=0).astype(BF)
-
-        @pl.when(height == group)
-        def _():
-            column_part[group] = plane_sum[group]
-
-        pl.when(height != group)(up_copy(group).start)
-
-    def down_copy(to):
-        return pltpu.make_async_remote_copy(
-            owned, gathered.at[height * 16 + spot], big_send.at[2], down_recv.at[height],
-            device_id=to, device_id_type=MESH,
-        )
-
-    def add_column():
-        big_wait(column_part, column_recv.at[0], 3)
-        owned[...] = jnp.sum(column_part[...].astype(F32), axis=0).astype(BF)
         for to in others:
-            down_copy(to).start()
-        gathered[height * 16 + spot] = owned[...]
+            pltpu.make_async_remote_copy(
+                plane_sum.at[group], column_part.at[group, height],
+                big_send.at[1], column_recv.at[group], device_id=to, device_id_type=MESH,
+            ).start()
+        column_part[group, height] = plane_sum[group]
 
     def spread(group):
+        big_wait(column_part.at[group], column_recv.at[group], 3)
         place_here = gathered.at[group * 16 + spot]
-
-        @pl.when(height != group)
-        def _():
-            pltpu.make_async_copy(place_here, place_here, down_recv.at[group]).wait()
-
+        place_here[...] = jnp.sum(column_part[group].astype(F32), axis=0).astype(BF)
         for h, w in around:
             pltpu.make_async_remote_copy(
-                place_here, place_here, big_send.at[3], gather_recv.at[group],
+                place_here, place_here, big_send.at[2], gather_recv.at[group],
                 device_id=(tm, h, w), device_id_type=MESH,
             ).start()
 
@@ -627,17 +607,13 @@
         pl.when(tm < 7)(to_previous(n).wait_recv)
     features_back(1)
     scatter_start(2)
-    pl.when((height == 3) | (height == 0))(add_column)
+    spread(3)
+    spread(0)
     add_plane(1)
     input_back(0)
     add_plane(2)
-    pl.when(height == 1)(add_column)
-    spread(3)
-    spread(0)
-    input_back(1)
-    pl.when(height == 2)(add_column)
     spread(1)
-    spread(2)
+    input_back(1, functools.partial(spread, 2))
 
     grad_scale = float(CELLS) ** -0.5
     chan_wait(1, chan_recv)
@@ -669,9 +645,8 @@
         core_copy(t).wait_send()
 
     big_wait(scatter, big_send.at[0], 60)
-    big_wait(plane_sum, big_send.at[1], 3)
-    big_wait(plane_sum, big_send.at[2], 3)
-    big_wait(gathered, big_send.at[3], 60)
+    big_wait(scatter, big_send.at[1], 12)
+    big_wait(gathered, big_send.at[2], 60)
     for group in range(4):
         swap_copy(group).wait_send()
         for copy in keep_copies(group):
@@ -743,8 +718,7 @@
             pltpu.VMEM((12 * C, 128), BF),
             pltpu.VMEM((CHIPS, PIECE, 128), BF),
             pltpu.VMEM((4, PIECE, 128), BF),
-            pltpu.VMEM((4, PIECE, 128), BF),
-            pltpu.VMEM((PIECE, 128), BF),
+            pltpu.VMEM((4, 4, PIECE, 128), BF),
             pltpu.VMEM((CHIPS, PIECE, 128), BF),
             pltpu.VMEM((CHIPS, PIECE, 128), BF),
             dma((12,)),
@@ -763,9 +737,8 @@
             dma((2,)),
             dma((12,)),
             dma((12,)),
+            dma((3,)),
             dma((4,)),
-            dma((4,)),
-            dma((1,)),
             dma((4,)),
             dma((4,)),
             dma((4,)),

time: 91.2 us -> 90.3 us (level)
  Pallas kernels: 90.2 us -> 89.2 us
    pallas_call x1, Pallas kernels: 84.9 us -> 84 us  [body(): pl.pallas_call(kernel, out_shape=(jax.ShapeDtypeStruct((4, 32, 32, C), BF...]
where the time goes in v1:
time: 90.3 us; the launch traced here: 90 us
  Pallas kernels  89.2 us (99%)
    pallas_call x1, Pallas kernels, body(): pl.pallas_call(kernel, out_shape=(jax.ShapeDtypeStruct((4, 32, 32, C), BF...  84 us
    pallas_call x1, Pallas kernels, body(): pl.pallas_call(finish, out_shape=(jax.ShapeDtypeStruct((4, 32, 32, C), BF...  5.28 us

profile of v1, /device:TPU:1, one launch (start us, length us, event | category | flops | bytes accessed | tf_op | source)
XLA Modules:
  0.0 90.0 jit_solution(16762690492328706212)
XLA Ops:
  0.6 84.0 %decoder_block_backward.1 = (bf16[4,32,32,256]{3,2,1,0:T(8,128)(2,1)}, bf16[64,48,128]{2,1,0:T(8,128)(2,1)}, bf16[64,48,128]{2,1,0:T(8,128)(2,1)}, f32[4,128]{1,0:T(4,128)}) custom-call(bf16[4,32,32,256]{3,2,1,0:T(8,128)(2,1)} %frames.1, bf16[2,32,32,256]{3,2,1,0:T(8,128)(2,1)} %history.1, bf16[4,32,32,256]{3,2,1,0:T(8,128)(2,1)} %cotangent.1, ...), custom_call_target="tpu_custom_call" | custom-call | tf_op jit(solution)/shard_map/decoder_block_backward/pallas_call | solution.py:683
  84.6 5.3 %scale_and_store.1 = (bf16[4,32,32,256]{3,2,1,0:T(8,128)(2,1)}, f32[9,256,256]{2,1,0:T(8,128)}, f32[3,256,256]{2,1,0:T(8,128)}, f32[1,256]{1,0:T(1,128)}, f32[1,256]{1,0:T(1,128)}) custom-call(bf16[4,32,32,256]{3,2,1,0:T(8,128)(2,1)} %get-tuple-element.14.grad_in, bf16[64,48,128]{2,1,0:T(8,128)(2,1)} %get-tuple-element.15.half, ...), custom_call_target="tpu_custom_call" | custom-call | tf_op jit(solution)/shard_map/scale_and_store/pallas_call | solution.py:761
